TPU v7x, 512 devices: a whole 4x4x16 slice. The times are simulated.
512 devices in a mesh: feat: 8 (over x, core), vert: 64 (over y, z).
Axes of the slice: x: 4, y: 4, z: 16, core: 2. Of those that a mesh axis runs over, the one named last changes fastest.
Arguments:
- features: bfloat16 [512, 131072], P('feat', 'vert'), may hold values from -6 to 6
- tiles: bfloat16 [64, 56, 128, 128], P('vert'), may hold values from -0.375 to 0.375
- tile_rows: int32 [64, 56], P('vert'), may hold values from 0 to 15, as said below
- tile_cols: int32 [64, 56], P('vert'), may hold values from 0 to 1023, as said below
- tile_counts: int32 [64], P('vert'), may hold values from 1 to 56, as said below
- weight: bfloat16 [512, 512], replicated, may hold values from -0.25 to 0.25
- output_gradient: bfloat16 [512, 131072], P(None, ('vert', 'feat')), may hold values from -6 to 6
Outputs:
- activation: bfloat16 [512, 131072], P(None, ('vert', 'feat'))
- weight_gradient: float32 [512, 512], replicated
- feature_grad: bfloat16 [512, 131072], P('feat', 'vert')
Inputs may be any that keep to these rules, and one draw needn't show every extreme that they name: `tile_rows`: slots at or beyond a block's count are unused; their tiles and indices are arbitrary. The block of a column tile, tile_cols // 16, equals the slot's own block or differs from it in exactly one of the lowest 4 bits. `tile_counts`: some block uses all 56 slots.
All inputs are finite; a program needn't handle non-finite values.
Results may differ from a plain program's by a relative error of at most 0.02.
Values may be sent and summed in bfloat16 or wider, within the bound.
A program may use at most 64 MiB of HBM per device.

v0:
```python
import jax
import jax.numpy as jnp
from jax import lax
from jax.sharding import PartitionSpec as P

LEVELS = 4


def partner(shard, axis, stride):
    return lax.ppermute(shard, axis, [(i, i ^ 1 << stride) for i in range(lax.axis_size(axis))])


def fetch_partners(features):
    fetched = []
    for bit in range(LEVELS):
        fetched.append(partner(features, "vert", bit))
    return fetched


def send_partials(remote_terms):
    received = []
    for bit in range(LEVELS):
        outgoing = remote_terms[:, bit].astype(jnp.bfloat16)
        received.append(partner(outgoing, "vert", bit).astype(jnp.float32))
    return received


def tile_products(stacked, level, local, rows, block_tiles, weights, row_tiles):
    picked = stacked[level, :, local]
    share_value = jnp.einsum(
        "cfk,crk->cfr", picked, block_tiles, preferred_element_type=jnp.float32
    )
    indicator_matrix = (rows[None, :] == jnp.arange(row_tiles, dtype=jnp.int32)[:, None]).astype(
        jnp.float32
    ) * weights[None, :]
    reduced_total = jnp.einsum("zy,yqw->qzw", indicator_matrix, share_value)
    return reduced_total.reshape(stacked.shape[1], row_tiles * stacked.shape[3])


def position_summands(share_value, slot_index, groups, feat_local, vdev):
    targets = jnp.arange(groups * (vdev // share_value.shape[2]), dtype=jnp.int32)
    placing = (slot_index[None, :] == targets[:, None]).astype(jnp.float32)
    return jnp.einsum("sc,cfk->fsk", placing, share_value).reshape(feat_local, groups, vdev)


def body(features, tiles, tile_rows, tile_cols, tile_counts, weight, output_gradient):
    feat_local, vdev = features.shape
    tile_side = tiles.shape[2]
    slot_count = tiles.shape[1]
    row_tiles = vdev // tile_side
    my_block = lax.axis_index("vert")
    block_tiles = tiles[0]
    rows = tile_rows[0]
    cols = tile_cols[0]
    differ = jnp.bitwise_xor(cols // row_tiles, my_block)
    level = jnp.zeros(cols.shape, jnp.int32)
    for bit in range(LEVELS):
        level = level + jnp.where(differ == 1 << bit, bit + 1, 0).astype(jnp.int32)
    local = cols % row_tiles
    valid = (jnp.arange(slot_count, dtype=jnp.int32) < tile_counts[0]).astype(jnp.float32)
    stacked = jnp.stack([features] + fetch_partners(features)).reshape(
        LEVELS + 1, feat_local, row_tiles, tile_side
    )
    aggregated = tile_products(stacked, level, local, rows, block_tiles, valid, row_tiles).astype(
        jnp.bfloat16
    )
    full_rows = lax.all_to_all(aggregated, "feat", split_axis=1, concat_axis=0, tiled=True)
    pre = jnp.einsum("io,iv->ov", weight, full_rows, preferred_element_type=jnp.float32)
    sigma = jax.nn.sigmoid(pre)
    activation = (pre * sigma).astype(jnp.bfloat16)
    pre_grad = (output_gradient.astype(jnp.float32) * sigma * (1.0 + pre * (1.0 - sigma))).astype(
        jnp.bfloat16
    )
    weight_term = jnp.einsum("iv,ov->io", full_rows, pre_grad, preferred_element_type=jnp.float32)
    weight_gradient = lax.psum(weight_term, ("feat", "vert"))
    agg_grad = jnp.einsum("io,ov->iv", weight, pre_grad, preferred_element_type=jnp.float32).astype(
        jnp.bfloat16
    )
    grad_cols = lax.all_to_all(agg_grad, "feat", split_axis=0, concat_axis=1, tiled=True)
    picked = grad_cols.reshape(feat_local, row_tiles, tile_side)[:, rows, :]
    share_value = (
        jnp.einsum("fcr,crk->cfk", picked, block_tiles, preferred_element_type=jnp.float32)
        * valid[:, None, None]
    )
    spread = position_summands(share_value, level * row_tiles + local, LEVELS + 1, feat_local, vdev)
    received = send_partials(spread[:, 1:])
    feature_grad = spread[:, 0]
    for term in received:
        feature_grad = feature_grad + term
    return (activation, weight_gradient, feature_grad.astype(jnp.bfloat16))


def solution(mesh):
    in_specs = (
        P("feat", "vert"),
        P("vert", None, None, None),
        P("vert", None),
        P("vert", None),
        P("vert"),
        P(),
        P(None, ("vert", "feat")),
    )
    out_specs = (P(None, ("vert", "feat")), P(), P("feat", "vert"))
    return jax.shard_map(body, mesh=mesh, in_specs=in_specs, out_specs=out_specs, check_vma=False)
```

profile of v0, /device:TPU:1, one launch (start us, length us, event | category | flops | bytes accessed | tf_op | source)
XLA Modules:
  0.0 628.8 jit_solution(14471863540489969215)
XLA Ops:
  7.2 5.9 collective-permute-start.1
  13.1 3.5 collective-permute-start
  16.6 12.7 %collective-permute-start.3 = (bf16[64,2048]{1,0:T(8,128)(2,1)}, bf16[64,2048]{1,0:T(8,128)(2,1)S(1)}, u32[]{:S(2)}, u32[]{:S(2)}) collective-permute-start(bf16[64,2048]{1,0:T(8,128)(2,1)} %param.7), channel_id=1, source_target_pairs={{0,8},{1,9},{2,10},{3,11},{4,12},{5,13},{6,14},{7,15},{8,0},{9,1},... | collective-permute-start | bytes 786440 | tf_op jit(solution)/shard_map/ppermute | solution.py:10
  29.4 4.0 collective-permute-start.2
  34.0 0.7 fusion.49
  34.7 1.0 copy.87
  35.7 0.8 copy_dynamic-update-slice_fusion.4
  36.6 10.2 %collective-permute-done.3 = bf16[64,2048]{1,0:T(8,128)(2,1)S(1)} collective-permute-done((bf16[64,2048]{1,0:T(8,128)(2,1)}, bf16[64,2048]{1,0:T(8,128)(2,1)S(1)}, u32[]{:S(2)}, u32[]{:S(2)}) %collective-permute-start.3) | collective-permute-done | bytes 262176 | tf_op jit(solution)/shard_map/ppermute | solution.py:10
  46.9 31.9 %collective-permute-done.2 = bf16[64,2048]{1,0:T(8,128)(2,1)S(1)} collective-permute-done((bf16[64,2048]{1,0:T(8,128)(2,1)}, bf16[64,2048]{1,0:T(8,128)(2,1)S(1)}, u32[]{:S(2)}, u32[]{:S(2)}) %collective-permute-start.2) | collective-permute-done | bytes 262176 | tf_op jit(solution)/shard_map/ppermute | solution.py:10
  78.8 0.8 copy_dynamic-update-slice_fusion.3
  79.5 0.8 copy_dynamic-update-slice_fusion.2
  80.3 0.8 copy_dynamic-update-slice_fusion.1
  81.0 0.8 copy_dynamic-update-slice_fusion
  81.8 2.2 gather_fusion
  84.1 1.4 fusion.2
  85.4 0.6 fusion.18
  86.0 0.1 convert_element_type.72
  86.1 0.8 copy.75
  86.9 4.8 all-to-all-start
  91.7 0.1 copy.76
  91.8 6.3 %all-to-all-done = bf16[64,8,256]{2,0,1:T(8,128)(2,1)S(1)} async-done(((bf16[64,8,256]{2,0,1:T(8,128)(2,1)}), bf16[64,8,256]{2,0,1:T(8,128)(2,1)S(1)}, u32[]{:S(2)}, u32[]{:S(2)}) %all-to-all-start) | async-done | bytes 262176 | tf_op jit(solution)/shard_map/all_to_all | solution.py:67
  98.2 1.2 multiply_convert_fusion
  99.4 0.3 fusion.17
  99.7 0.8 copy.77
  100.6 4.4 all-to-all-start.1
  105.0 6.5 %all-to-all-done.1 = bf16[8,64,256]{2,1,0:T(8,128)(2,1)S(1)} async-done(((bf16[8,64,256]{2,1,0:T(8,128)(2,1)}), bf16[8,64,256]{2,1,0:T(8,128)(2,1)S(1)}, u32[]{:S(2)}, u32[]{:S(2)}) %all-to-all-start.1) | async-done | bytes 262176 | tf_op jit(solution)/shard_map/all_to_all | solution.py:79
  111.5 0.1 copy.78
  111.6 0.1 reshape.231
  111.8 0.7 gather_fusion.1
  112.5 0.6 fusion.11
  113.1 2.4 fusion.8
  115.5 4.4 reshape.232
  119.9 2.5 convert.6
  122.4 1.9 fusion.51
  124.3 0.2 copy.115
  124.5 0.2 copy.112
  124.6 0.9 copy.113
  125.5 0.9 copy.114
  126.3 1.9 collective-permute-start.5
  128.3 1.9 collective-permute-start.6
  130.2 8.5 %collective-permute-start.7 = (bf16[64,2048]{1,0:T(8,128)(2,1)S(1)}, bf16[64,2048]{1,0:T(8,128)(2,1)}, u32[]{:S(2)}, u32[]{:S(2)}) collective-permute-start(bf16[64,2048]{1,0:T(8,128)(2,1)S(1)} %bitcast.108), channel_id=1, source_target_pairs={{0,8},{1,9},{2,10},{3,11},{4,12},{5,13},{6,14},{7,15},{8,0},{9,1},... | collective-permute-start | bytes 786440 | tf_op jit(solution)/shard_map/ppermute | solution.py:10
  138.7 5.8 collective-permute-start.4
  144.5 1.3 fusion.52
  145.8 1.8 copy.81
  147.7 33.5 %collective-permute-done.6 = bf16[64,2048]{1,0:T(8,128)(2,1)} collective-permute-done((bf16[64,2048]{1,0:T(8,128)(2,1)}, bf16[64,2048]{1,0:T(8,128)(2,1)}, u32[]{:S(2)}, u32[]{:S(2)}) %collective-permute-start.6) | collective-permute-done | bytes 262176 | tf_op jit(solution)/shard_map/ppermute | solution.py:10
  181.2 2.2 fusion.25
  183.3 436.4 %all-reduce.2.cloned.1.call-done = f32[512,512]{1,0:T(8,128)} async-done(((f32[512,512]{1,0:T(8,128)}), f32[512,512]{1,0:T(8,128)}) %all-reduce.2.cloned.1.call-update) | async-done | bytes 1048592 | tf_op jit(solution)/shard_map/psum | solution.py:75
  619.7 2.3 copy.122
  (28 shorter events, 0.3 us)
Async XLA Ops:
  7.2 76.9 %copy-start = (bf16[1,56,128,128]{3,2,1,0:T(8,128)(2,1)S(1)}, bf16[1,56,128,128]{3,2,1,0:T(8,128)(2,1)}, u32[]{:S(2)}) copy-start(bf16[1,56,128,128]{3,2,1,0:T(8,128)(2,1)} %param.8) | copy-start | bytes 5505028
  7.2 29.3 %collective-permute-start.1 = (bf16[64,2048]{1,0:T(8,128)(2,1)}, bf16[64,2048]{1,0:T(8,128)(2,1)S(1)}, u32[]{:S(2)}, u32[]{:S(2)}) collective-permute-start(bf16[64,2048]{1,0:T(8,128)(2,1)} %param.7), channel_id=1, source_target_pairs={{0,2},{1,3},{2,0},{3,1},{4,6},{5,7},{6,4},{7,5},{8,10},{9,11},{10,... | collective-permute-start | bytes 786440 | tf_op jit(solution)/shard_map/ppermute | solution.py:10
  13.1 23.5 %collective-permute-start = (bf16[64,2048]{1,0:T(8,128)(2,1)}, bf16[64,2048]{1,0:T(8,128)(2,1)S(1)}, u32[]{:S(2)}, u32[]{:S(2)}) collective-permute-start(bf16[64,2048]{1,0:T(8,128)(2,1)} %param.7), channel_id=1, source_target_pairs={{0,1},{1,0},{2,3},{3,2},{4,5},{5,4},{6,7},{7,6},{8,9},{9,8},{10,11... | collective-permute-start | bytes 786440 | tf_op jit(solution)/shard_map/ppermute | solution.py:10
  16.6 30.2 %collective-permute-start.3 = (bf16[64,2048]{1,0:T(8,128)(2,1)}, bf16[64,2048]{1,0:T(8,128)(2,1)S(1)}, u32[]{:S(2)}, u32[]{:S(2)}) collective-permute-start(bf16[64,2048]{1,0:T(8,128)(2,1)} %param.7), channel_id=1, source_target_pairs={{0,8},{1,9},{2,10},{3,11},{4,12},{5,13},{6,14},{7,15},{8,0},{9,1},... | collective-permute-start | bytes 786440 | tf_op jit(solution)/shard_map/ppermute | solution.py:10
  29.4 49.4 %collective-permute-start.2 = (bf16[64,2048]{1,0:T(8,128)(2,1)}, bf16[64,2048]{1,0:T(8,128)(2,1)S(1)}, u32[]{:S(2)}, u32[]{:S(2)}) collective-permute-start(bf16[64,2048]{1,0:T(8,128)(2,1)} %param.7), channel_id=1, source_target_pairs={{0,4},{1,5},{2,6},{3,7},{4,0},{5,1},{6,2},{7,3},{8,12},{9,13},{10,... | collective-permute-start | bytes 786440 | tf_op jit(solution)/shard_map/ppermute | solution.py:10
  84.0 1.4 copy-start.3
  85.4 6.2 copy-start.2
  86.0 12.1 %copy-start.1 = (bf16[512,512]{1,0:T(8,128)(2,1)S(1)}, bf16[512,512]{1,0:T(8,128)(2,1)}, u32[]{:S(2)}) copy-start(bf16[512,512]{1,0:T(8,128)(2,1)} %param.12) | copy-start | bytes 1572868
  86.9 11.3 %all-to-all-start = ((bf16[64,8,256]{2,0,1:T(8,128)(2,1)}), bf16[64,8,256]{2,0,1:T(8,128)(2,1)S(1)}, u32[]{:S(2)}, u32[]{:S(2)}) async-start(bf16[64,8,256]{2,0,1:T(8,128)(2,1)} %copy.75), calls=%async_computation | async-start | bytes 524288 | tf_op jit(solution)/shard_map/all_to_all | solution.py:67
  99.4 5.6 copy-start.4
  100.6 10.9 %all-to-all-start.1 = ((bf16[8,64,256]{2,1,0:T(8,128)(2,1)}), bf16[8,64,256]{2,1,0:T(8,128)(2,1)S(1)}, u32[]{:S(2)}, u32[]{:S(2)}) async-start(bf16[8,64,256]{2,1,0:T(8,128)(2,1)} %bitcast.12), calls=%async_computation.1 | async-start | bytes 524288 | tf_op jit(solution)/shard_map/all_to_all | solution.py:79
  104.9 514.8 %all-reduce.2.cloned.1.call-start = ((), (), s32[]{:S(2)}) async-start(), calls=%async_computation.2 | async-start | bytes 2097152 | tf_op jit(solution)/shard_map/psum | solution.py:75
  126.3 21.3 %collective-permute-start.5 = (bf16[64,2048]{1,0:T(8,128)(2,1)}, bf16[64,2048]{1,0:T(8,128)(2,1)}, u32[]{:S(2)}, u32[]{:S(2)}) collective-permute-start(bf16[64,2048]{1,0:T(8,128)(2,1)} %bitcast.96), channel_id=1, source_target_pairs={{0,2},{1,3},{2,0},{3,1},{4,6},{5,7},{6,4},{7,5},{8,10},{9,11},{10,... | collective-permute-start | bytes 786440 | tf_op jit(solution)/shard_map/ppermute | solution.py:10
  128.3 52.9 %collective-permute-start.6 = (bf16[64,2048]{1,0:T(8,128)(2,1)}, bf16[64,2048]{1,0:T(8,128)(2,1)}, u32[]{:S(2)}, u32[]{:S(2)}) collective-permute-start(bf16[64,2048]{1,0:T(8,128)(2,1)} %bitcast.95), channel_id=1, source_target_pairs={{0,4},{1,5},{2,6},{3,7},{4,0},{5,1},{6,2},{7,3},{8,12},{9,13},{10,... | collective-permute-start | bytes 786440 | tf_op jit(solution)/shard_map/ppermute | solution.py:10
  130.2 50.9 %collective-permute-start.7 = (bf16[64,2048]{1,0:T(8,128)(2,1)S(1)}, bf16[64,2048]{1,0:T(8,128)(2,1)}, u32[]{:S(2)}, u32[]{:S(2)}) collective-permute-start(bf16[64,2048]{1,0:T(8,128)(2,1)S(1)} %bitcast.108), channel_id=1, source_target_pairs={{0,8},{1,9},{2,10},{3,11},{4,12},{5,13},{6,14},{7,15},{8,0},{9,1},... | collective-permute-start | bytes 786440 | tf_op jit(solution)/shard_map/ppermute | solution.py:10
  138.7 42.4 %collective-permute-start.4 = (bf16[64,2048]{1,0:T(8,128)(2,1)S(1)}, bf16[64,2048]{1,0:T(8,128)(2,1)}, u32[]{:S(2)}, u32[]{:S(2)}) collective-permute-start(bf16[64,2048]{1,0:T(8,128)(2,1)S(1)} %bitcast.107), channel_id=1, source_target_pairs={{0,1},{1,0},{2,3},{3,2},{4,5},{5,4},{6,7},{7,6},{8,9},{9,8},{10,11... | collective-permute-start | bytes 786440 | tf_op jit(solution)/shard_map/ppermute | solution.py:10
  145.8 35.3 %slice-start = ((f32[64,5,2048]{2,1,0:T(8,128)}), f32[64,1,2048]{2,1,0:T(1,128)S(1)}, s32[]{:S(2)}) async-start(f32[64,5,2048]{2,1,0:T(8,128)} %reshape.232), calls=%async_computation.3 | async-start | bytes 1048576 | tf_op jit(solution)/shard_map/slice | solution.py:87
Sparse Core Ops, SparseCore 0:
  146.0 473.7 all-reduce.1
where the time goes:
time: 630 us; the launch traced here: 629 us
  waiting for transfers between devices  525 us (83%)
  starting transfers between devices  53.5 us (8%)
  local copies, waits for them, and re-layouts  22.5 us (4%)
  between operations  14.9 us (2%)
  matrix products  7.74 us (1%)
    psum x1, waiting for transfers between devices, body(): weight_gradient = lax.psum(weight_term, ('feat', 'vert'))  436 us
    ppermute x8, waiting for transfers between devices, partner(): lax.ppermute(shard, axis, [(i, i ^ 1 << stride) for i in range(lax.axis_s...  75.5 us
    ppermute x8, starting transfers between devices, partner(): lax.ppermute(shard, axis, [(i, i ^ 1 << stride) for i in range(lax.axis_s...  44.3 us
  transfers between devices with their start and end apart: 11, of which 6 were waited for; matrix products, arithmetic and copies ran while one was open for 1% of the time, Pallas kernels for 0%

commit v1 on v0

--- a/solution.py
+++ b/solution.py
@@ -4,6 +4,11 @@
 from jax.sharding import PartitionSpec as P
 
 LEVELS = 4
+
+
+def by_each_axis(array, first, second):
+    inner = lax.psum(array, first)
+    return lax.psum(inner, second)
 
 
 def partner(shard, axis, stride):
@@ -72,7 +77,7 @@
         jnp.bfloat16
     )
     weight_term = jnp.einsum("iv,ov->io", full_rows, pre_grad, preferred_element_type=jnp.float32)
-    weight_gradient = lax.psum(weight_term, ("feat", "vert"))
+    weight_gradient = by_each_axis(weight_term, "vert", "feat")
     agg_grad = jnp.einsum("io,ov->iv", weight, pre_grad, preferred_element_type=jnp.float32).astype(
         jnp.bfloat16
     )

time: 630 us -> 499 us (0.79)
  waiting for transfers between devices: 525 us -> 393 us
    psum x1 -> x2, waiting for transfers between devices: 436 us -> 340 us  [the longest x1 260 us: by_each_axis(): inner = lax.psum(array, first)]
    ppermute x8, waiting for transfers between devices: 75.5 us -> 41.4 us  [partner(): lax.ppermute(shard, axis, [(i, i ^ 1 << stride) for i in range(lax.axis_s...]
  transfers between devices with their start and end apart: 11 -> 12, of which waited for: 6 -> 6; matrix products, arithmetic and copies ran while one was open for 1% -> 5% of each run, Pallas kernels for 0% -> 0%
where the time goes in v1:
time: 499 us; the launch traced here: 497 us
  waiting for transfers between devices  393 us (79%)
  starting transfers between devices  53.5 us (11%)
  local copies, waits for them, and re-layouts  22.5 us (5%)
  between operations  15 us (3%)
  matrix products  7.74 us (2%)
  other arithmetic  5.94 us (1%)
    psum x1, waiting for transfers between devices, by_each_axis(): inner = lax.psum(array, first)  260 us
    psum x1, waiting for transfers between devices, by_each_axis(): return lax.psum(inner, second)  79.2 us
    ppermute x8, starting transfers between devices, partner(): lax.ppermute(shard, axis, [(i, i ^ 1 << stride) for i in range(lax.axis_s...  44.3 us
    ppermute x8, waiting for transfers between devices, partner(): lax.ppermute(shard, axis, [(i, i ^ 1 << stride) for i in range(lax.axis_s...  41.4 us
    unnamed x26, local copies, waits for them, and re-layouts  10.5 us
  transfers between devices with their start and end apart: 12, of which 6 were waited for; matrix products, arithmetic and copies ran while one was open for 5% of the time, Pallas kernels for 0%

profile of v1, /device:TPU:1, one launch (start us, length us, event | category | flops | bytes accessed | tf_op | source)
XLA Modules:
  0.0 497.2 jit_solution(14834941330735500032)
XLA Ops:
  7.2 5.9 %collective-permute-start.1 = (bf16[64,2048]{1,0:T(8,128)(2,1)}, bf16[64,2048]{1,0:T(8,128)(2,1)S(1)}, u32[]{:S(2)}, u32[]{:S(2)}) collective-permute-start(bf16[64,2048]{1,0:T(8,128)(2,1)} %param.7), channel_id=1, source_target_pairs={{0,2},{1,3},{2,0},{3,1},{4,6},{5,7},{6,4},{7,5},{8,10},{9,11},{10,... | collective-permute-start | bytes 786440 | tf_op jit(solution)/shard_map/ppermute | solution.py:15
  13.1 3.5 collective-permute-start
  16.6 12.7 %collective-permute-start.3 = (bf16[64,2048]{1,0:T(8,128)(2,1)}, bf16[64,2048]{1,0:T(8,128)(2,1)S(1)}, u32[]{:S(2)}, u32[]{:S(2)}) collective-permute-start(bf16[64,2048]{1,0:T(8,128)(2,1)} %param.7), channel_id=1, source_target_pairs={{0,8},{1,9},{2,10},{3,11},{4,12},{5,13},{6,14},{7,15},{8,0},{9,1},... | collective-permute-start | bytes 786440 | tf_op jit(solution)/shard_map/ppermute | solution.py:15
  29.4 4.0 collective-permute-start.2
  34.0 0.7 fusion.47
  34.7 0.7 fusion.49
  35.4 1.0 copy.87
  36.4 0.8 copy_dynamic-update-slice_fusion.4
  37.2 9.6 %collective-permute-done.3 = bf16[64,2048]{1,0:T(8,128)(2,1)S(1)} collective-permute-done((bf16[64,2048]{1,0:T(8,128)(2,1)}, bf16[64,2048]{1,0:T(8,128)(2,1)S(1)}, u32[]{:S(2)}, u32[]{:S(2)}) %collective-permute-start.3) | collective-permute-done | bytes 262176 | tf_op jit(solution)/shard_map/ppermute | solution.py:15
  46.9 31.9 %collective-permute-done.2 = bf16[64,2048]{1,0:T(8,128)(2,1)S(1)} collective-permute-done((bf16[64,2048]{1,0:T(8,128)(2,1)}, bf16[64,2048]{1,0:T(8,128)(2,1)S(1)}, u32[]{:S(2)}, u32[]{:S(2)}) %collective-permute-start.2) | collective-permute-done | bytes 262176 | tf_op jit(solution)/shard_map/ppermute | solution.py:15
  78.8 0.8 copy_dynamic-update-slice_fusion.3
  79.5 0.8 copy_dynamic-update-slice_fusion.2
  80.3 0.8 copy_dynamic-update-slice_fusion.1
  81.0 0.8 copy_dynamic-update-slice_fusion
  81.8 2.2 gather_fusion
  84.1 1.4 fusion.2
  85.4 0.6 fusion.18
  86.1 0.8 copy.75
  86.9 4.8 all-to-all-start
  91.7 0.1 copy.76
  91.9 6.3 %all-to-all-done = bf16[64,8,256]{2,0,1:T(8,128)(2,1)S(1)} async-done(((bf16[64,8,256]{2,0,1:T(8,128)(2,1)}), bf16[64,8,256]{2,0,1:T(8,128)(2,1)S(1)}, u32[]{:S(2)}, u32[]{:S(2)}) %all-to-all-start) | async-done | bytes 262176 | tf_op jit(solution)/shard_map/all_to_all | solution.py:72
  98.2 1.2 multiply_convert_fusion
  99.4 0.3 fusion.17
  99.7 0.8 copy.77
  100.6 4.4 all-to-all-start.1
  104.9 1.3 fusion.52
  106.3 5.2 %all-to-all-done.1 = bf16[8,64,256]{2,1,0:T(8,128)(2,1)S(1)} async-done(((bf16[8,64,256]{2,1,0:T(8,128)(2,1)}), bf16[8,64,256]{2,1,0:T(8,128)(2,1)S(1)}, u32[]{:S(2)}, u32[]{:S(2)}) %all-to-all-start.1) | async-done | bytes 262176 | tf_op jit(solution)/shard_map/all_to_all | solution.py:84
  111.5 0.1 copy.78
  111.6 0.1 reshape.231
  111.8 0.7 gather_fusion.1
  112.5 0.6 fusion.11
  113.1 2.4 fusion.8
  115.5 4.4 reshape.232
  119.9 2.6 convert.6
  122.4 1.9 fusion.51
  124.4 0.2 copy.115
  124.5 0.2 copy.112
  124.7 0.9 copy.113
  125.5 0.8 copy.114
  126.4 1.9 collective-permute-start.5
  128.3 1.9 collective-permute-start.6
  130.2 8.5 %collective-permute-start.7 = (bf16[64,2048]{1,0:T(8,128)(2,1)S(1)}, bf16[64,2048]{1,0:T(8,128)(2,1)}, u32[]{:S(2)}, u32[]{:S(2)}) collective-permute-start(bf16[64,2048]{1,0:T(8,128)(2,1)S(1)} %bitcast.108), channel_id=1, source_target_pairs={{0,8},{1,9},{2,10},{3,11},{4,12},{5,13},{6,14},{7,15},{8,0},{9,1},... | collective-permute-start | bytes 786440 | tf_op jit(solution)/shard_map/ppermute | solution.py:15
  138.7 5.8 %collective-permute-start.4 = (bf16[64,2048]{1,0:T(8,128)(2,1)S(1)}, bf16[64,2048]{1,0:T(8,128)(2,1)}, u32[]{:S(2)}, u32[]{:S(2)}) collective-permute-start(bf16[64,2048]{1,0:T(8,128)(2,1)S(1)} %bitcast.107), channel_id=1, source_target_pairs={{0,1},{1,0},{2,3},{3,2},{4,5},{5,4},{6,7},{7,6},{8,9},{9,8},{10,11... | collective-permute-start | bytes 786440 | tf_op jit(solution)/shard_map/ppermute | solution.py:15
  144.5 260.4 %all-reduce.3.cloned.1.call-done = f32[512,512]{1,0:T(8,128)} async-done(((f32[512,512]{1,0:T(8,128)}), f32[512,512]{1,0:T(8,128)}) %all-reduce.3.cloned.1.call-update) | async-done | bytes 1048592 | tf_op jit(solution)/shard_map/psum | solution.py:10
  404.9 1.8 copy.81
  406.8 2.0 fusion.25
  408.8 79.2 %all-reduce.5.cloned.1.call-done = f32[512,512]{1,0:T(8,128)} async-done(((f32[512,512]{1,0:T(8,128)}), f32[512,512]{1,0:T(8,128)}) %all-reduce.5.cloned.1.call-update) | async-done | bytes 1048592 | tf_op jit(solution)/shard_map/psum | solution.py:11
  488.1 2.3 copy.123
  (31 shorter events, 0.5 us)
Async XLA Ops:
  7.2 76.9 %copy-start = (bf16[1,56,128,128]{3,2,1,0:T(8,128)(2,1)S(1)}, bf16[1,56,128,128]{3,2,1,0:T(8,128)(2,1)}, u32[]{:S(2)}) copy-start(bf16[1,56,128,128]{3,2,1,0:T(8,128)(2,1)} %param.8) | copy-start | bytes 5505028
  7.2 30.0 %collective-permute-start.1 = (bf16[64,2048]{1,0:T(8,128)(2,1)}, bf16[64,2048]{1,0:T(8,128)(2,1)S(1)}, u32[]{:S(2)}, u32[]{:S(2)}) collective-permute-start(bf16[64,2048]{1,0:T(8,128)(2,1)} %param.7), channel_id=1, source_target_pairs={{0,2},{1,3},{2,0},{3,1},{4,6},{5,7},{6,4},{7,5},{8,10},{9,11},{10,... | collective-permute-start | bytes 786440 | tf_op jit(solution)/shard_map/ppermute | solution.py:15
  13.1 24.1 %collective-permute-start = (bf16[64,2048]{1,0:T(8,128)(2,1)}, bf16[64,2048]{1,0:T(8,128)(2,1)S(1)}, u32[]{:S(2)}, u32[]{:S(2)}) collective-permute-start(bf16[64,2048]{1,0:T(8,128)(2,1)} %param.7), channel_id=1, source_target_pairs={{0,1},{1,0},{2,3},{3,2},{4,5},{5,4},{6,7},{7,6},{8,9},{9,8},{10,11... | collective-permute-start | bytes 786440 | tf_op jit(solution)/shard_map/ppermute | solution.py:15
  16.6 30.2 %collective-permute-start.3 = (bf16[64,2048]{1,0:T(8,128)(2,1)}, bf16[64,2048]{1,0:T(8,128)(2,1)S(1)}, u32[]{:S(2)}, u32[]{:S(2)}) collective-permute-start(bf16[64,2048]{1,0:T(8,128)(2,1)} %param.7), channel_id=1, source_target_pairs={{0,8},{1,9},{2,10},{3,11},{4,12},{5,13},{6,14},{7,15},{8,0},{9,1},... | collective-permute-start | bytes 786440 | tf_op jit(solution)/shard_map/ppermute | solution.py:15
  29.4 49.4 %collective-permute-start.2 = (bf16[64,2048]{1,0:T(8,128)(2,1)}, bf16[64,2048]{1,0:T(8,128)(2,1)S(1)}, u32[]{:S(2)}, u32[]{:S(2)}) collective-permute-start(bf16[64,2048]{1,0:T(8,128)(2,1)} %param.7), channel_id=1, source_target_pairs={{0,4},{1,5},{2,6},{3,7},{4,0},{5,1},{6,2},{7,3},{8,12},{9,13},{10,... | collective-permute-start | bytes 786440 | tf_op jit(solution)/shard_map/ppermute | solution.py:15
  84.0 1.4 copy-start.3
  85.4 6.3 %copy-start.2 = (bf16[512,256]{1,0:T(8,128)(2,1)S(1)}, bf16[512,256]{1,0:T(8,128)(2,1)}, u32[]{:S(2)}) copy-start(bf16[512,256]{1,0:T(8,128)(2,1)} %param.13) | copy-start | bytes 786436
  86.0 5.8 %copy-start.4 = (s32[1,56]{1,0:T(1,128)S(1)}, s32[1,56]{1,0:T(1,128)}, u32[]{:S(2)}) copy-start(s32[1,56]{1,0:T(1,128)} %param.10) | copy-start | bytes 676
  86.0 12.2 %copy-start.1 = (bf16[512,512]{1,0:T(8,128)(2,1)S(1)}, bf16[512,512]{1,0:T(8,128)(2,1)}, u32[]{:S(2)}) copy-start(bf16[512,512]{1,0:T(8,128)(2,1)} %param.12) | copy-start | bytes 1572868
  86.9 11.3 %all-to-all-start = ((bf16[64,8,256]{2,0,1:T(8,128)(2,1)}), bf16[64,8,256]{2,0,1:T(8,128)(2,1)S(1)}, u32[]{:S(2)}, u32[]{:S(2)}) async-start(bf16[64,8,256]{2,0,1:T(8,128)(2,1)} %copy.75), calls=%async_computation | async-start | bytes 524288 | tf_op jit(solution)/shard_map/all_to_all | solution.py:72
  100.6 10.9 %all-to-all-start.1 = ((bf16[8,64,256]{2,1,0:T(8,128)(2,1)}), bf16[8,64,256]{2,1,0:T(8,128)(2,1)S(1)}, u32[]{:S(2)}, u32[]{:S(2)}) async-start(bf16[8,64,256]{2,1,0:T(8,128)(2,1)} %bitcast.12), calls=%async_computation.1 | async-start | bytes 524288 | tf_op jit(solution)/shard_map/all_to_all | solution.py:84
  104.9 300.0 %all-reduce.3.cloned.1.call-start = ((), (), s32[]{:S(2)}) async-start(), calls=%async_computation.2 | async-start | bytes 2097152 | tf_op jit(solution)/shard_map/psum | solution.py:10
  106.2 381.8 %all-reduce.5.cloned.1.call-start = ((), (), s32[]{:S(2)}) async-start(), calls=%async_computation.3 | async-start | bytes 2097152 | tf_op jit(solution)/shard_map/psum | solution.py:11
  126.4 280.4 %collective-permute-start.5 = (bf16[64,2048]{1,0:T(8,128)(2,1)}, bf16[64,2048]{1,0:T(8,128)(2,1)S(1)}, u32[]{:S(2)}, u32[]{:S(2)}) collective-permute-start(bf16[64,2048]{1,0:T(8,128)(2,1)} %bitcast.96), channel_id=1, source_target_pairs={{0,2},{1,3},{2,0},{3,1},{4,6},{5,7},{6,4},{7,5},{8,10},{9,11},{10,... | collective-permute-start | bytes 786440 | tf_op jit(solution)/shard_map/ppermute | solution.py:15
  128.3 278.5 %collective-permute-start.6 = (bf16[64,2048]{1,0:T(8,128)(2,1)}, bf16[64,2048]{1,0:T(8,128)(2,1)S(1)}, u32[]{:S(2)}, u32[]{:S(2)}) collective-permute-start(bf16[64,2048]{1,0:T(8,128)(2,1)} %bitcast.95), channel_id=1, source_target_pairs={{0,4},{1,5},{2,6},{3,7},{4,0},{5,1},{6,2},{7,3},{8,12},{9,13},{10,... | collective-permute-start | bytes 786440 | tf_op jit(solution)/shard_map/ppermute | solution.py:15
  130.2 276.6 %collective-permute-start.7 = (bf16[64,2048]{1,0:T(8,128)(2,1)S(1)}, bf16[64,2048]{1,0:T(8,128)(2,1)}, u32[]{:S(2)}, u32[]{:S(2)}) collective-permute-start(bf16[64,2048]{1,0:T(8,128)(2,1)S(1)} %bitcast.108), channel_id=1, source_target_pairs={{0,8},{1,9},{2,10},{3,11},{4,12},{5,13},{6,14},{7,15},{8,0},{9,1},... | collective-permute-start | bytes 786440 | tf_op jit(solution)/shard_map/ppermute | solution.py:15
  138.7 268.1 %collective-permute-start.4 = (bf16[64,2048]{1,0:T(8,128)(2,1)S(1)}, bf16[64,2048]{1,0:T(8,128)(2,1)}, u32[]{:S(2)}, u32[]{:S(2)}) collective-permute-start(bf16[64,2048]{1,0:T(8,128)(2,1)S(1)} %bitcast.107), channel_id=1, source_target_pairs={{0,1},{1,0},{2,3},{3,2},{4,5},{5,4},{6,7},{7,6},{8,9},{9,8},{10,11... | collective-permute-start | bytes 786440 | tf_op jit(solution)/shard_map/ppermute | solution.py:15
  404.9 1.9 slice-start
Sparse Core Ops, SparseCore 0:
  109.7 295.1 all-reduce.2
  407.4 80.6 all-reduce.4
